TPU v7x, 1024 devices: a whole 8x8x8 slice. The times are simulated.
1024 devices in a mesh: group: 16 (over y_hi, z), expert: 16 (over x, core), tp: 4 (over y_lo).
Axes of the slice: x: 8, y: 8 (y_hi: 2, y_lo: 4; y = y_hi * 4 + y_lo), z: 8, core: 2. Of those that a mesh axis runs over, the one named last changes fastest.
Arguments:
- grad_out: bfloat16 [4096, 3584], P(('group', 'expert'), 'tp'), may hold values from -2 to 2
- route_weights: bfloat16 [4096, 8], P(('group', 'expert')), may hold values from 0.19921875 to 2.5
- expert_ids: int32 [4096, 8], P(('group', 'expert')), may hold values from 0 to 127, as said below
- w_gate: bfloat16 [256, 3584, 512], P(('group', 'expert'), None, 'tp'), may hold values from -0.09375 to 0.09375
- w_up: bfloat16 [256, 3584, 512], P(('group', 'expert'), None, 'tp'), may hold values from -0.09375 to 0.09375
- w_down: bfloat16 [256, 512, 3584], P(('group', 'expert'), 'tp'), may hold values from -0.09375 to 0.09375
- saved_gate: bfloat16 [131072, 512], P(('group', 'expert'), 'tp'), may hold values from -5 to 5
- saved_up: bfloat16 [131072, 512], P(('group', 'expert'), 'tp'), may hold values from -5 to 5
Outputs:
- grad_in: float32 [4096, 3584], P(('group', 'expert'), 'tp')
- grad_route: float32 [4096, 8], P(('group', 'expert'))
Inputs may be any that keep to these rules, and one draw needn't show every extreme that they name: `expert_ids`: each row names 8 different experts, two in each of 4 of the 8 node groups (expert e lies in node group e // 16); among the 16 tokens of one device no expert is named more than 2 times, and some device reaches 2.
All inputs are finite; a program needn't handle non-finite values.
Results may differ from a plain program's by a relative error of at most 0.014.
Values may be sent and summed in bfloat16 or wider, within the bound.
A program may use at most 32 MiB of HBM per device.

v0:
```python
import jax
import jax.numpy as jnp
from jax import lax
from jax.sharding import PartitionSpec as P


def contract_last(left_side, right_side):
    return lax.dot_general(
        left_side, right_side, (((1,), (1,)), ((), ())), preferred_element_type=jnp.float32
    )


def shards(grad_out, route_weights, expert_ids, w_gate, w_up, w_down, saved_gate, saved_up):
    tokens_here = grad_out.shape[0]
    width_here = grad_out.shape[1]
    topk_here = expert_ids.shape[1]
    n_group = lax.axis_size("group")
    n_expert = lax.axis_size("expert")
    positions = n_group * n_expert
    slot_count = saved_gate.shape[0]
    most_here = slot_count // positions
    pair_count = tokens_here * topk_here
    highest = lax.Precision.HIGHEST
    flat_ids = expert_ids.reshape(pair_count)
    owner_token = jnp.arange(pair_count, dtype=jnp.int32) // topk_here
    same_expert = flat_ids[:, None] == flat_ids[None, :]
    earlier = owner_token[None, :] < owner_token[:, None]
    rank_of = jnp.sum(jnp.logical_and(same_expert, earlier).astype(jnp.int32), axis=1)
    weights_f32 = route_weights.astype(jnp.float32)
    position_index = jnp.arange(positions, dtype=jnp.int32)
    hits = (position_index[None, None, :] // 2 == expert_ids[:, :, None]).astype(jnp.float32)
    hits_grid = hits.reshape(tokens_here, topk_here, n_group, n_expert)
    level_plus = (rank_of.reshape(tokens_here, topk_here) + 1).astype(jnp.float32)
    codes = jnp.einsum("ik,ikge->gie", level_plus, hits_grid, precision=highest).astype(
        jnp.bfloat16
    )
    scales = jnp.einsum("ik,ikge->gie", weights_f32, hits_grid, precision=highest).astype(
        jnp.bfloat16
    )
    named = jnp.sum(hits_grid, axis=(1, 3)) > 0.5
    rows_out = jnp.where(
        named.T[:, :, None], grad_out[None, :, :], jnp.zeros_like(grad_out)[None, :, :]
    )
    rows_in, codes_in, scales_in = (
        lax.all_to_all(rows_out, "group", split_axis=0, concat_axis=0, tiled=True),
        lax.all_to_all(codes, "group", split_axis=0, concat_axis=0, tiled=True),
        lax.all_to_all(scales, "group", split_axis=0, concat_axis=0, tiled=True),
    )
    level_value = jnp.arange(most_here, dtype=jnp.float32) + 1.0
    select = codes_in.astype(jnp.float32)[:, :, :, None] == level_value[None, None, None, :]
    fanned = jnp.einsum(
        "giem,gid->gemd", select.astype(jnp.bfloat16), rows_in, preferred_element_type=jnp.float32
    ).astype(jnp.bfloat16)
    inbound = lax.all_to_all(fanned, "expert", split_axis=1, concat_axis=1, tiled=True)
    routed_rows = inbound.reshape(slot_count, width_here)
    down_local = w_down[0]
    adjoint = contract_last(lax.all_gather(routed_rows, "tp", axis=1, tiled=True), down_local)
    gate_pre = saved_gate.astype(jnp.float32)
    up_pre = saved_up.astype(jnp.float32)
    gate_sigmoid = jax.nn.sigmoid(gate_pre)
    activated = gate_pre * gate_sigmoid
    route_part = jnp.sum(activated * up_pre * adjoint, axis=1)
    route_slot = lax.psum(route_part, "tp")
    d_gate = (adjoint * up_pre * gate_sigmoid * (1.0 + gate_pre * (1.0 - gate_sigmoid))).astype(
        jnp.bfloat16
    )
    d_up = (adjoint * activated).astype(jnp.bfloat16)
    gate_local = w_gate[0]
    up_local = w_up[0]
    partial_terms = contract_last(d_gate, gate_local) + contract_last(d_up, up_local)
    summed = lax.psum_scatter(
        partial_terms.astype(jnp.bfloat16), "tp", scatter_dimension=1, tiled=True
    ).astype(jnp.float32)
    quarter = summed.shape[1]
    going_back = summed.reshape(n_group, n_expert, most_here, quarter)
    route_back = route_slot.reshape(n_group, n_expert, most_here)
    back_rows, back_route = (
        lax.all_to_all(
            going_back.astype(jnp.bfloat16), "expert", split_axis=1, concat_axis=1, tiled=True
        ).astype(going_back.dtype),
        lax.all_to_all(
            route_back.astype(jnp.bfloat16), "expert", split_axis=1, concat_axis=1, tiled=True
        ).astype(route_back.dtype),
    )
    select_f32 = select.astype(jnp.float32)
    weighted_select = select_f32 * scales_in.astype(jnp.float32)[:, :, :, None]
    presum = jnp.einsum("giem,gemd->gid", weighted_select, back_rows, precision=highest)
    route_presum = jnp.einsum("giem,gem->gie", select_f32, back_route, precision=highest)
    came_rows, came_route = (
        lax.all_to_all(
            presum.astype(jnp.bfloat16), "group", split_axis=0, concat_axis=0, tiled=True
        ).astype(presum.dtype),
        lax.all_to_all(
            route_presum.astype(jnp.bfloat16), "group", split_axis=0, concat_axis=0, tiled=True
        ).astype(route_presum.dtype),
    )
    grad_in = jnp.sum(came_rows, axis=0)
    grad_route = jnp.einsum("gie,ikge->ik", came_route, hits_grid, precision=highest)
    return (grad_in, grad_route)


def solution(mesh):
    return jax.shard_map(
        shards,
        mesh=mesh,
        in_specs=(
            P(("group", "expert"), "tp"),
            P(("group", "expert"), None),
            P(("group", "expert"), None),
            P(("group", "expert"), None, "tp"),
            P(("group", "expert"), None, "tp"),
            P(("group", "expert"), "tp", None),
            P(("group", "expert"), "tp"),
            P(("group", "expert"), "tp"),
        ),
        out_specs=(P(("group", "expert"), "tp"), P(("group", "expert"), None)),
        check_vma=False,
    )
```

profile of v0, /device:TPU:32, one launch (start us, length us, event | category | flops | bytes accessed | tf_op | source)
XLA Modules:
  0.0 354.1 jit_solution(10838893634239652896)
XLA Ops:
  7.2 0.8 copy.33
  9.3 0.7 reshape.110
  10.0 20.7 %all-to-all-start = ((bf16[16,2,128]{2,1,0:T(2,128)(2,1)}), bf16[16,2,128]{2,1,0:T(2,128)(2,1)S(1)}, u32[]{:S(2)}, u32[]{:S(2)}) async-start(bf16[16,2,128]{2,1,0:T(2,128)(2,1)} %reshape.110), calls=%async_computation | async-start | bytes 16384 | tf_op jit(solution)/shard_map/all_to_all | solution.py:46
  31.1 1.6 broadcast_select_fusion
  32.7 10.2 %all-to-all-done = bf16[16,2,128]{2,1,0:T(2,128)(2,1)S(1)} async-done(((bf16[16,2,128]{2,1,0:T(2,128)(2,1)}), bf16[16,2,128]{2,1,0:T(2,128)(2,1)S(1)}, u32[]{:S(2)}, u32[]{:S(2)}) %all-to-all-start) | async-done | bytes 8224 | tf_op jit(solution)/shard_map/all_to_all | solution.py:46
  43.0 3.6 %all-to-all-start.2 = ((bf16[16,16,896]{2,1,0:T(8,128)(2,1)}), bf16[16,16,896]{2,1,0:T(8,128)(2,1)S(1)}, u32[]{:S(2)}, u32[]{:S(2)}) async-start(bf16[16,16,896]{2,1,0:T(8,128)(2,1)} %broadcast_select_fusion), calls=%async_computation.2 | async-start | bytes 917504 | tf_op jit(solution)/shard_map/all_to_all | solution.py:45
  46.7 18.2 %all-to-all-done.2 = bf16[16,16,896]{2,1,0:T(8,128)(2,1)S(1)} async-done(((bf16[16,16,896]{2,1,0:T(8,128)(2,1)}), bf16[16,16,896]{2,1,0:T(8,128)(2,1)S(1)}, u32[]{:S(2)}, u32[]{:S(2)}) %all-to-all-start.2) | async-done | bytes 458784 | tf_op jit(solution)/shard_map/all_to_all | solution.py:45
  65.5 0.7 copy.37
  66.2 31.7 %all_to_all.40 = bf16[16,16,2,896]{3,2,0,1:T(2,128)(2,1)S(1)} all-to-all(bf16[16,16,2,896]{3,2,0,1:T(2,128)(2,1)S(1)} %copy.37), channel_id=1, replica_groups=mesh['group'=16,'expert'=16,'tp'=4] {'expert'}, dimensions={1} | all-to-all | bytes 1835008 | tf_op jit(solution)/shard_map/all_to_all | solution.py:54
  98.6 1.3 reshape.96
  100.1 71.8 %all-gather.2.cloned.1.call-done = bf16[512,3584]{1,0:T(8,128)(2,1)} async-done(((bf16[512,896]{1,0:T(8,128)(2,1)}), bf16[512,3584]{1,0:T(8,128)(2,1)}) %all-gather.2.cloned.1.call-update) | async-done | bytes 3670032 | tf_op jit(solution)/shard_map/all_gather | solution.py:57
  172.0 3.4 fusion.17
  175.3 1.2 fusion.2
  176.5 3.0 add_convert_fusion
  179.5 5.9 %copy.66 = bf16[512,3584]{0,1:T(8,128)(2,1)} copy(bf16[512,3584]{1,0:T(8,128)(2,1)} %add_convert_fusion) | data formatting | bytes 7340032
  186.6 0.7 reshape.112
  187.3 10.5 %all-to-all-start.1 = ((bf16[16,2,128]{2,1,0:T(2,128)(2,1)}), bf16[16,2,128]{2,1,0:T(2,128)(2,1)S(1)}, u32[]{:S(2)}, u32[]{:S(2)}) async-start(bf16[16,2,128]{2,1,0:T(2,128)(2,1)} %reshape.112), calls=%async_computation.1 | async-start | bytes 16384 | tf_op jit(solution)/shard_map/all_to_all | solution.py:47
  197.8 10.6 %psum.7 = bf16[512]{0:T(512)(128)(2,1)S(1)} all-reduce(f32[512]{0:T(512)S(1)} %get-tuple-element.2), channel_id=1, replica_groups=mesh['group'=16,'expert'=16,'tp'=4] {'tp'}, use_global_device_ids=true, to_apply=%region_5.6 | all-reduce | flops 512 | bytes 3072 | tf_op jit(solution)/shard_map/psum | solution.py:63
  208.6 0.8 copy.43
  209.4 0.7 all-to-all-done.1
  210.1 7.1 %all-to-all-start.6 = ((bf16[16,16,2]{0,2,1:T(2,128)(2,1)}), bf16[16,16,2]{0,2,1:T(2,128)(2,1)S(1)}, u32[]{:S(2)}, u32[]{:S(2)}) async-start(bf16[16,16,2]{0,2,1:T(2,128)(2,1)} %copy.43), calls=%async_computation.6 | async-start | bytes 16384 | tf_op jit(solution)/shard_map/all_to_all | solution.py:81
  217.2 48.8 %reduce-scatter.4.cloned.1.call-done = bf16[896,512]{1,0:T(8,128)(2,1)} async-done(((bf16[3584,512]{1,0:T(8,128)(2,1)}), bf16[896,512]{1,0:T(8,128)(2,1)}) %reduce-scatter.4.cloned.1.call-update) | async-done | bytes 917520
  265.9 1.5 copy.67
  267.8 1.6 copy.41
  269.4 6.8 %all-to-all-start.4 = ((bf16[16,16,2,896]{3,2,0,1:T(2,128)(2,1)}), bf16[16,16,2,896]{3,2,0,1:T(2,128)(2,1)S(1)}, u32[]{:S(2)}, u32[]{:S(2)}) async-start(bf16[16,16,2,896]{3,2,0,1:T(2,128)(2,1)} %copy.41), calls=%async_computation.4 | async-start | bytes 1835008 | tf_op jit(solution)/shard_map/all_to_all | solution.py:78
  276.6 0.7 reshape.114
  277.3 22.5 %all-to-all-done.4 = bf16[16,16,2,896]{3,2,0,1:T(2,128)(2,1)S(1)} async-done(((bf16[16,16,2,896]{3,2,0,1:T(2,128)(2,1)}), bf16[16,16,2,896]{3,2,0,1:T(2,128)(2,1)S(1)}, u32[]{:S(2)}, u32[]{:S(2)}) %all-to-all-start.4) | async-done | bytes 917536 | tf_op jit(solution)/shard_map/all_to_all | solution.py:78
  299.8 10.6 %all-to-all-start.7 = ((bf16[16,2,128]{2,1,0:T(2,128)(2,1)}), bf16[16,2,128]{2,1,0:T(2,128)(2,1)S(1)}, u32[]{:S(2)}, u32[]{:S(2)}) async-start(bf16[16,2,128]{2,1,0:T(2,128)(2,1)} %reshape.114), calls=%async_computation.7 | async-start | bytes 16384 | tf_op jit(solution)/shard_map/all_to_all | solution.py:93
  310.4 1.6 fusion
  312.0 10.7 %all-to-all-done.7 = bf16[16,2,128]{2,1,0:T(2,128)(2,1)S(1)} async-done(((bf16[16,2,128]{2,1,0:T(2,128)(2,1)}), bf16[16,2,128]{2,1,0:T(2,128)(2,1)S(1)}, u32[]{:S(2)}, u32[]{:S(2)}) %all-to-all-start.7) | async-done | bytes 8224 | tf_op jit(solution)/shard_map/all_to_all | solution.py:93
  322.7 3.6 %all-to-all-start.5 = ((bf16[16,16,896]{2,1,0:T(8,128)(2,1)}), bf16[16,16,896]{2,1,0:T(8,128)(2,1)S(1)}, u32[]{:S(2)}, u32[]{:S(2)}) async-start(bf16[16,16,896]{2,1,0:T(8,128)(2,1)} %fusion), calls=%async_computation.5 | async-start | bytes 917504 | tf_op jit(solution)/shard_map/all_to_all | solution.py:90
  327.7 18.9 %all-to-all-done.5 = bf16[16,16,896]{2,1,0:T(8,128)(2,1)S(1)} async-done(((bf16[16,16,896]{2,1,0:T(8,128)(2,1)}), bf16[16,16,896]{2,1,0:T(8,128)(2,1)S(1)}, u32[]{:S(2)}, u32[]{:S(2)}) %all-to-all-start.5) | async-done | bytes 458784 | tf_op jit(solution)/shard_map/all_to_all | solution.py:90
  (53 shorter events, 7.3 us)
Async XLA Ops:
  7.2 168.2 %copy-start = (bf16[1,3584,128]{2,1,0:T(8,128)(2,1)S(1)}, bf16[1,3584,128]{2,1,0:T(8,128)(2,1)}, u32[]{:S(2)}) copy-start(bf16[1,3584,128]{2,1,0:T(8,128)(2,1)} %param.11) | copy-start | bytes 2752516
  10.0 33.0 %all-to-all-start = ((bf16[16,2,128]{2,1,0:T(2,128)(2,1)}), bf16[16,2,128]{2,1,0:T(2,128)(2,1)S(1)}, u32[]{:S(2)}, u32[]{:S(2)}) async-start(bf16[16,2,128]{2,1,0:T(2,128)(2,1)} %reshape.110), calls=%async_computation | async-start | bytes 16384 | tf_op jit(solution)/shard_map/all_to_all | solution.py:46
  43.0 22.0 %all-to-all-start.2 = ((bf16[16,16,896]{2,1,0:T(8,128)(2,1)}), bf16[16,16,896]{2,1,0:T(8,128)(2,1)S(1)}, u32[]{:S(2)}, u32[]{:S(2)}) async-start(bf16[16,16,896]{2,1,0:T(8,128)(2,1)} %broadcast_select_fusion), calls=%async_computation.2 | async-start | bytes 917504 | tf_op jit(solution)/shard_map/all_to_all | solution.py:45
  46.5 125.4 %all-gather.2.cloned.1.call-start = ((), (), s32[]{:S(2)}) async-start(), calls=%async_computation.9 | async-start | bytes 4587520 | tf_op jit(solution)/shard_map/all_gather | solution.py:57
  66.2 33.7 %copy-start.2 = (bf16[512,128]{1,0:T(8,128)(2,1)S(1)}, bf16[512,128]{1,0:T(8,128)(2,1)}, u32[]{:S(2)}) copy-start(bf16[512,128]{1,0:T(8,128)(2,1)} %param.14) | copy-start | bytes 393220
  66.2 33.8 %copy-start.3 = (bf16[512,128]{1,0:T(8,128)(2,1)S(1)}, bf16[512,128]{1,0:T(8,128)(2,1)}, u32[]{:S(2)}) copy-start(bf16[512,128]{1,0:T(8,128)(2,1)} %param.15) | copy-start | bytes 393220
  66.2 105.8 %copy-start.5 = (bf16[1,128,3584]{2,1,0:T(8,128)(2,1)S(1)}, bf16[1,128,3584]{2,1,0:T(8,128)(2,1)}, u32[]{:S(2)}) copy-start(bf16[1,128,3584]{2,1,0:T(8,128)(2,1)} %param.13) | copy-start | bytes 2752516
  99.8 166.1 %reduce-scatter.4.cloned.1.call-start = ((), (), s32[]{:S(2)}) async-start(), calls=%async_computation.10 | async-start | bytes 4587520
  175.3 1.2 copy-start.1
  185.5 0.7 copy-start.4
  187.3 22.8 %all-to-all-start.1 = ((bf16[16,2,128]{2,1,0:T(2,128)(2,1)}), bf16[16,2,128]{2,1,0:T(2,128)(2,1)S(1)}, u32[]{:S(2)}, u32[]{:S(2)}) async-start(bf16[16,2,128]{2,1,0:T(2,128)(2,1)} %reshape.112), calls=%async_computation.1 | async-start | bytes 16384 | tf_op jit(solution)/shard_map/all_to_all | solution.py:47
  210.1 59.3 %all-to-all-start.6 = ((bf16[16,16,2]{0,2,1:T(2,128)(2,1)}), bf16[16,16,2]{0,2,1:T(2,128)(2,1)S(1)}, u32[]{:S(2)}, u32[]{:S(2)}) async-start(bf16[16,16,2]{0,2,1:T(2,128)(2,1)} %copy.43), calls=%async_computation.6 | async-start | bytes 16384 | tf_op jit(solution)/shard_map/all_to_all | solution.py:81
  269.4 30.4 %all-to-all-start.4 = ((bf16[16,16,2,896]{3,2,0,1:T(2,128)(2,1)}), bf16[16,16,2,896]{3,2,0,1:T(2,128)(2,1)S(1)}, u32[]{:S(2)}, u32[]{:S(2)}) async-start(bf16[16,16,2,896]{3,2,0,1:T(2,128)(2,1)} %copy.41), calls=%async_computation.4 | async-start | bytes 1835008 | tf_op jit(solution)/shard_map/all_to_all | solution.py:78
  299.8 22.9 %all-to-all-start.7 = ((bf16[16,2,128]{2,1,0:T(2,128)(2,1)}), bf16[16,2,128]{2,1,0:T(2,128)(2,1)S(1)}, u32[]{:S(2)}, u32[]{:S(2)}) async-start(bf16[16,2,128]{2,1,0:T(2,128)(2,1)} %reshape.114), calls=%async_computation.7 | async-start | bytes 16384 | tf_op jit(solution)/shard_map/all_to_all | solution.py:93
  322.7 23.9 %all-to-all-start.5 = ((bf16[16,16,896]{2,1,0:T(8,128)(2,1)}), bf16[16,16,896]{2,1,0:T(8,128)(2,1)S(1)}, u32[]{:S(2)}, u32[]{:S(2)}) async-start(bf16[16,16,896]{2,1,0:T(8,128)(2,1)} %fusion), calls=%async_computation.5 | async-start | bytes 917504 | tf_op jit(solution)/shard_map/all_to_all | solution.py:90
Sparse Core Ops, SparseCore 0:
  100.0 71.9 all-gather.1
  185.6 80.2 reduce-scatter.3
where the time goes:
time: 355 us; the launch traced here: 354 us
  waiting for transfers between devices  202 us (57%)
  starting transfers between devices  62.9 us (18%)
  blocking collectives  42.3 us (12%)
  local copies, waits for them, and re-layouts  18.5 us (5%)
  between operations  14.4 us (4%)
  matrix products  10.5 us (3%)
  other arithmetic  3.69 us (1%)
    all_gather x1, waiting for transfers between devices, shards(): lax.all_gather(routed_rows, 'tp', axis=1, tiled=True)  71.8 us
    unnamed x3, waiting for transfers between devices  48.8 us
    all_to_all x1, blocking collectives, shards(): lax.all_to_all(fanned, 'expert', split_axis=1, concat_axis=1, tiled=True)  31.7 us
    all_to_all x1, waiting for transfers between devices, shards(): lax.all_to_all(going_back.astype(jnp.bfloat16), 'expert', split_axis=1, c...  22.5 us
    all_to_all x1, starting transfers between devices, shards(): lax.all_to_all(codes, 'group', split_axis=0, concat_axis=0, tiled=True)  20.7 us
    all_to_all x1, waiting for transfers between devices, shards(): lax.all_to_all(presum.astype(jnp.bfloat16), 'group', split_axis=0, concat...  18.9 us
    all_to_all x1, waiting for transfers between devices, shards(): lax.all_to_all(rows_out, 'group', split_axis=0, concat_axis=0, tiled=True)  18.2 us
    unnamed x27, local copies, waits for them, and re-layouts  11.9 us
  transfers between devices with their start and end apart: 9, of which 8 were waited for; matrix products, arithmetic and copies ran while one was open for 3% of the time, Pallas kernels for 0%

commit v1 on v0

v1 whole, which is shorter than its diff:
```python
import functools

import jax
import jax.numpy as jnp
from jax import lax
from jax.experimental import pallas as pl
from jax.experimental.pallas import tpu as pltpu
from jax.sharding import PartitionSpec as P

MESH = pl.DeviceIdType.MESH
F32 = jnp.float32
BF16 = jnp.bfloat16
TP = 4
TOK = 16
META = 128


def dot_nn(left, right):
    return lax.dot_general(left, right, (((1,), (0,)), ((), ())), preferred_element_type=F32)


def dot_nt(left, right):
    return lax.dot_general(left, right, (((1,), (1,)), ((), ())), preferred_element_type=F32)


def rcopy(src, dst, send, recv, device):
    return pltpu.make_async_remote_copy(
        src_ref=src, dst_ref=dst, send_sem=send, recv_sem=recv, device_id=device, device_id_type=MESH
    )


def step_of(j, count):
    odd = j % 2
    return odd * ((j + 1) // 2) + (1 - odd) * ((count - j // 2) % count)


def kernel(
    nx, nz, width,
    tok, wg_hbm, wu_hbm, wd_hbm, sg_hbm, su_hbm,
    gin_ref, grt_ref,
    T, SEL, SMAT, SWT, IDW, RH, WD, WG, WU, SG, SU, A1, A2, A3, TM, RT, RTS, RTR, ZTS, ZTR,
    SR, SL, RR, RL, ZS, ZRET, OUT, XR, HS, HB, HR,
    lsem, ws, wr, hs, hr, xs, xr, zs, zr, ags, agr, rss, rsr, zbs, zbr, rts, rtr, zts, ztr, xbs, xbr,
):
    g = lax.axis_index("group")
    e = lax.axis_index("expert")
    q = lax.axis_index("tp")
    h, z = g // nz, g % nz
    x, c = e // 2, e % 2
    nb = 2 * nx
    ntok = nb * TOK
    sp = 2 * nb
    nslot = nz * sp
    hid = 128

    def dev_x(k):
        return {"expert": ((x + k) % nx) * 2 + c}

    def dev_z(zz):
        return {"group": h * nz + zz}

    sibling = {"expert": x * 2 + (1 - c)}
    partner = {"group": (1 - h) * nz + z}

    pairs = (
        (sg_hbm, SG.at[0], SG.at[1]),
        (su_hbm, SU.at[0], SU.at[1]),
        (wd_hbm.at[0], WD.at[pl.ds(0, hid), :], WD.at[pl.ds(hid, hid), :]),
        (wg_hbm.at[0], WG.at[:, pl.ds(0, hid)], WG.at[:, pl.ds(hid, hid)]),
        (wu_hbm.at[0], WU.at[:, pl.ds(0, hid)], WU.at[:, pl.ds(hid, hid)]),
    )
    local = [pltpu.make_async_copy(src, own, lsem.at[i]) for i, (src, own, _) in enumerate(pairs)]
    for copy in local:
        copy.start()

    barrier = pltpu.get_barrier_semaphore()
    for k in range(1, nx):
        pl.semaphore_signal(barrier, inc=1, device_id=dev_x(k), device_id_type=MESH)
    for k in range(1, nz):
        pl.semaphore_signal(barrier, inc=1, device_id=dev_z((z + k) % nz), device_id_type=MESH)
    for k in range(1, TP):
        pl.semaphore_signal(barrier, inc=1, device_id={"tp": (q + k) % TP}, device_id_type=MESH)
    pl.semaphore_signal(barrier, inc=1, device_id=sibling, device_id_type=MESH)
    pl.semaphore_signal(barrier, inc=1, device_id=partner, device_id_type=MESH)
    pl.semaphore_wait(barrier, nx + nz + TP - 1)

    to_partner = rcopy(tok, T.at[x, h], hs.at[0], hr.at[0], partner)
    to_partner.start()
    own_x = [rcopy(tok, T.at[x, h], xs.at[0, k], xr.at[h, x], dev_x(k)) for k in range(1, nx)]
    for copy in own_x:
        copy.start()
    T[x, h] = tok[...]
    siblings = [rcopy(src, far, ws.at[i], wr.at[i], sibling) for i, (src, _, far) in enumerate(pairs)]
    for copy in siblings:
        copy.start()
    rcopy(tok, T.at[x, 1 - h], hs.at[0], hr.at[0], partner).wait_recv()
    far_x = [
        rcopy(T.at[x, 1 - h], T.at[x, 1 - h], xs.at[1, k], xr.at[1 - h, x], dev_x(k)) for k in range(1, nx)
    ]
    for copy in far_x:
        copy.start()

    for i in range(2):
        local[i].wait()
        siblings[i].wait_recv()
    row = lax.broadcasted_iota(jnp.int32, (nslot, 8 * nx * nz), 0)
    col = lax.broadcasted_iota(jnp.int32, (nslot, 8 * nx * nz), 1)
    j_of, rest = row // sp, row % sp
    z_of = (z + step_of(j_of, nz)) % nz
    where_of = ((((rest // 2) % 2) * nz + z_of) * nx + rest // 4) * 4 + c * 2 + rest % 2
    pick = (where_of == col).astype(F32).astype(BF16)
    for s in range(2):
        gate = dot_nn(pick, SG[s])
        up = dot_nn(pick, SU[s])
        sigma = jax.nn.sigmoid(gate)
        act = gate * sigma
        lanes = pl.ds(s * hid, hid)
        A1[:, :, lanes] = (up * sigma * (1.0 + gate * (1.0 - sigma))).reshape(nz, sp, hid)
        A2[:, :, lanes] = act.reshape(nz, sp, hid)
        A3[:, :, lanes] = (act * up).reshape(nz, sp, hid)

    for hb in range(2):
        for k in range(1, nx):
            src_x = (x + k) % nx
            rcopy(T.at[src_x, hb], T.at[src_x, hb], xs.at[0, k], xr.at[hb, src_x], dev_x(k)).wait_recv()

    meta = T[:, :, :, pl.ds(width, META)].reshape(ntok, META).astype(F32)
    meta_t = jnp.transpose(meta)
    IDW[...] = meta_t[0:16, :]
    ids8 = IDW[0:8, :]
    w8 = IDW[8:16, :]

    def expert_at(j):
        zz = (z + nz - step_of(j, nz)) % nz
        return ((h * nz + zz) * nx + x).astype(F32)

    match_rows, weight_rows = [], []
    for j in range(nz):
        hit = (ids8 == expert_at(j)).astype(F32)
        match_rows.append(jnp.sum(hit, axis=0, keepdims=True))
        weight_rows.append(jnp.sum(hit * w8, axis=0, keepdims=True))
    t_row = lax.broadcasted_iota(jnp.int32, (ntok, ntok), 0)
    t_col = lax.broadcasted_iota(jnp.int32, (ntok, ntok), 1)
    before = jnp.logical_and(t_row // TOK == t_col // TOK, t_row < t_col).astype(F32).astype(BF16)
    matches = jnp.concatenate(match_rows, axis=0)
    ranks = dot_nn(matches.astype(BF16), before)
    s_row = lax.broadcasted_iota(jnp.int32, (sp, ntok), 0)
    s_block = (s_row // 2 == lax.broadcasted_iota(jnp.int32, (sp, ntok), 1) // TOK).astype(F32)
    s_level = (s_row % 2).astype(F32)
    for j in range(nz):
        chosen = s_block * matches[j:j + 1, :] * (s_level == ranks[j:j + 1, :]).astype(F32)
        SMAT[j] = chosen
    tokens = T[:, :, :, pl.ds(0, width)].reshape(ntok, width)
    selected = dot_nn(SMAT[...].reshape(nslot, ntok).astype(BF16), tokens).astype(BF16)
    SEL[...] = selected.reshape(nz, sp, width)
    for j in range(1, nz):
        zz = (z + nz - step_of(j, nz)) % nz
        rcopy(SEL.at[j], RH.at[q, j], zs.at[j], zr.at[j], dev_z(zz)).start()
    RH[q, 0] = SEL[0]
    weighted = jnp.concatenate([SMAT[j] * weight_rows[j] for j in range(nz)], axis=0)
    SWT[...] = jnp.transpose(weighted).astype(BF16)

    for i in range(2, 5):
        local[i].wait()
        siblings[i].wait_recv()

    def spread(origin, j, way):
        return rcopy(
            RH.at[origin, j], RH.at[origin, j], ags.at[way, origin, j], agr.at[origin, j],
            {"tp": (q + 1 - 2 * way) % TP},
        )

    def passed(s, j, way):
        src, dst = ((SR, RR), (SL, RL))[way]
        return rcopy(
            src.at[s, j], dst.at[s, j], rss.at[way, s, j], rsr.at[way, s, j], {"tp": (q + 1 - 2 * way) % TP}
        )

    def back(j):
        return rcopy(ZS.at[j], ZRET.at[j], zbs.at[j], zbr.at[j], dev_z((z + step_of(j, nz)) % nz))

    def route_tp(k):
        return rcopy(RTS, RTR.at[k - 1], rts.at[k - 1], rtr.at[k - 1], {"tp": (q + k) % TP})

    def route_z(j):
        return rcopy(ZTS, ZTR.at[j], zts.at[j], ztr.at[j], dev_z((z + step_of(j, nz)) % nz))

    def body(t, carry):
        @pl.when(t < nz)
        def _():
            @pl.when(t > 0)
            def _():
                rcopy(SEL.at[t], RH.at[q, t], zs.at[t], zr.at[t], dev_z(z)).wait_recv()

            @pl.when(q < TP - 1)
            def _():
                spread(q, t, 0).start()

            @pl.when(q > 0)
            def _():
                spread(q, t, 1).start()

        for k in range(1, TP):
            j = t - k

            @pl.when(jnp.logical_and(j >= 0, j < nz))
            def _():
                @pl.when(q >= k)
                def _():
                    spread(q - k, j, 0).wait_recv()

                    @pl.when(q < TP - 1)
                    def _():
                        spread(q - k, j, 0).start()

                @pl.when(q + k < TP)
                def _():
                    spread(q + k, j, 1).wait_recv()

                    @pl.when(q > 0)
                    def _():
                        spread(q + k, j, 1).start()

        j = t - (TP - 1)

        @pl.when(jnp.logical_and(j >= 0, j < nz))
        def _():
            adjoint = dot_nt(RH[0, j], WD[:, pl.ds(0, width)])
            for s in range(1, TP):
                adjoint += dot_nt(RH[s, j], WD[:, pl.ds(s * width, width)])
            d_gate = (adjoint * A1[j]).astype(BF16)
            d_up = (adjoint * A2[j]).astype(BF16)
            RT[j] = jnp.broadcast_to(jnp.sum(adjoint * A3[j], axis=1, keepdims=True), (sp, META))
            for s in range(TP):
                part = pl.ds(s * width, width)
                TM[s, j] = dot_nt(d_gate, WG[part, :]) + dot_nt(d_up, WU[part, :])

        @pl.when(t == nz + TP - 2)
        def _():
            RTS[...] = jnp.transpose(RT[...].reshape(nslot, META))[0:8, :]
            for k in range(1, TP):
                route_tp(k).start()

        @pl.when(t == nz + TP - 1)
        def _():
            for k in range(1, TP):
                route_tp(k).wait_recv()
            ZTS[...] = RTS[...] + RTR[0] + RTR[1] + RTR[2]
            ZTR[0] = ZTS[...]
            for i in range(1, nz):
                route_z(i).start()

        for k in range(TP - 1):
            j = t - (TP - 1) - k

            @pl.when(jnp.logical_and(j >= 0, j < nz))
            def _():
                for way in range(2):
                    place = k if way == 0 else TP - 1 - k
                    src, dst = ((SR, RR), (SL, RL))[way]
                    targets = range(TP - 1, k, -1) if way == 0 else range(0, TP - 1 - k)

                    @pl.when(q == place)
                    def _():
                        for s in targets:
                            value = TM[s, j]
                            if k > 0:
                                passed(s, j, way).wait_recv()
                                value = value + dst[s, j].astype(F32)
                            src[s, j] = value.astype(BF16)
                            passed(s, j, way).start()

        j = t - 2 * (TP - 1)

        @pl.when(jnp.logical_and(j >= 0, j < nz))
        def _():
            @pl.when(q > 0)
            def _():
                passed(q, j, 0).wait_recv()
                TM[q, j] = TM[q, j] + RR[q, j].astype(F32)

            @pl.when(q < TP - 1)
            def _():
                passed(q, j, 1).wait_recv()
                TM[q, j] = TM[q, j] + RL[q, j].astype(F32)

            @pl.when(j == 0)
            def _():
                ZRET[0] = TM[q, j].astype(BF16)

            @pl.when(j > 0)
            def _():
                ZS[j] = TM[q, j].astype(BF16)
                back(j).start()

        return carry

    lax.fori_loop(0, nz + 2 * (TP - 1), body, 0)

    for j in range(1, nz):
        route_z(j).wait_recv()
    columns = jnp.transpose(ZTR[...].reshape(nz * 8, nslot))
    ids_now = IDW[0:8, :]
    route = jnp.zeros((8, ntok), F32)
    for j in range(nz):
        column = columns[j * sp:(j + 1) * sp, 8 * j:8 * j + 1]
        value = jnp.sum(SMAT[j] * column, axis=0, keepdims=True)
        route += (ids_now == expert_at(j)).astype(F32) * value
    route_t = jnp.transpose(jnp.concatenate([route, jnp.zeros((META - 8, ntok), F32)], axis=0))
    OUT[:, :, :, pl.ds(width, META)] = route_t.astype(BF16).reshape(nx, 2, TOK, META)

    for j in range(1, nz):
        back(j).wait_recv()
    combined = dot_nn(SWT[...], ZRET[...].reshape(nslot, width)).astype(BF16)
    OUT[:, :, :, pl.ds(0, width)] = combined.reshape(nx, 2, TOK, width)

    def home(k):
        to = (x + k) % nx
        return rcopy(OUT.at[to], XR.at[k], xbs.at[k], xbr.at[k], dev_x(k))

    for k in range(1, nx):
        home(k).start()
    total = OUT[x].astype(F32)
    for k in range(1, nx):
        home(k).wait_recv()
        total += XR[k].astype(F32)
    HS[...] = total
    HB[...] = HS[1 - h].astype(BF16)
    homeward = rcopy(HB, HR, hs.at[1], hr.at[1], partner)
    homeward.start()
    homeward.wait_recv()
    result = HS[h] + HR[...].astype(F32)
    gin_ref[...] = result[:, 0:width]
    grt_ref[...] = result[:, width:width + 8]

    to_partner.wait_send()
    homeward.wait_send()
    for copy in own_x + far_x + siblings:
        copy.wait_send()
    for k in range(1, TP):
        route_tp(k).wait_send()
    for k in range(1, nx):
        home(k).wait_send()
    for j in range(1, nz):
        rcopy(SEL.at[j], RH.at[q, j], zs.at[j], zr.at[j], dev_z(z)).wait_send()
        back(j).wait_send()
        route_z(j).wait_send()

    def drain(j, carry):
        for origin in range(TP):
            @pl.when(jnp.logical_and(q >= origin, q < TP - 1))
            def _():
                spread(origin, j, 0).wait_send()

            @pl.when(jnp.logical_and(q <= origin, q > 0))
            def _():
                spread(origin, j, 1).wait_send()

            @pl.when(q < origin)
            def _():
                passed(origin, j, 0).wait_send()

            @pl.when(q > origin)
            def _():
                passed(origin, j, 1).wait_send()

        return carry

    lax.fori_loop(0, nz, drain, 0)


def shards(grad_out, route_weights, expert_ids, w_gate, w_up, w_down, saved_gate, saved_up):
    width = grad_out.shape[1]
    nz = lax.axis_size("group") // 2
    nx = lax.axis_size("expert") // 2
    nb = 2 * nx
    ntok, sp = nb * TOK, 2 * nb
    nslot = nz * sp
    features = TP * width
    slots = saved_gate.shape[0]
    topk = expert_ids.shape[1]
    tok = jnp.concatenate(
        [grad_out, expert_ids.astype(BF16), route_weights, jnp.zeros((TOK, META - 2 * topk), BF16)], axis=1
    )
    vmem = pltpu.VMEM
    dma = pltpu.SemaphoreType.DMA
    scratch = [
        vmem((nx, 2, TOK, width + META), BF16),
        vmem((nz, sp, width), BF16),
        vmem((nz, sp, ntok), F32),
        vmem((ntok, nslot), BF16),
        vmem((16, ntok), F32),
        vmem((TP, nz, sp, width), BF16),
        vmem((256, features), BF16),
        vmem((features, 256), BF16),
        vmem((features, 256), BF16),
        vmem((2, slots, 128), BF16),
        vmem((2, slots, 128), BF16),
        vmem((nz, sp, 256), F32),
        vmem((nz, sp, 256), F32),
        vmem((nz, sp, 256), F32),
        vmem((TP, nz, sp, width), F32),
        vmem((nz, sp, META), F32),
        vmem((8, nslot), F32),
        vmem((TP - 1, 8, nslot), F32),
        vmem((8, nslot), F32),
        vmem((nz, 8, nslot), F32),
        vmem((TP, nz, sp, width), BF16),
        vmem((TP, nz, sp, width), BF16),
        vmem((TP, nz, sp, width), BF16),
        vmem((TP, nz, sp, width), BF16),
        vmem((nz, sp, width), BF16),
        vmem((nz, sp, width), BF16),
        vmem((nx, 2, TOK, width + META), BF16),
        vmem((nx, 2, TOK, width + META), BF16),
        vmem((2, TOK, width + META), F32),
        vmem((TOK, width + META), BF16),
        vmem((TOK, width + META), BF16),
        dma((5,)), dma((5,)), dma((5,)),
        dma((2,)), dma((2,)),
        dma((2, nx)), dma((2, nx)),
        dma((nz,)), dma((nz,)),
        dma((2, TP, nz)), dma((TP, nz)),
        dma((2, TP, nz)), dma((2, TP, nz)),
        dma((nz,)), dma((nz,)),
        dma((TP - 1,)), dma((TP - 1,)),
        dma((nz,)), dma((nz,)),
        dma((nx,)), dma((nx,)),
    ]
    whole = pl.BlockSpec(memory_space=pltpu.VMEM)
    far = pl.BlockSpec(memory_space=pl.ANY)
    return pl.pallas_call(
        functools.partial(kernel, nx, nz, width),
        out_shape=(
            jax.ShapeDtypeStruct((TOK, width), F32),
            jax.ShapeDtypeStruct((TOK, topk), F32),
        ),
        in_specs=[whole] + [far] * 5,
        out_specs=(whole, whole),
        scratch_shapes=scratch,
        compiler_params=pltpu.CompilerParams(
            collective_id=0, has_side_effects=True, vmem_limit_bytes=48 * 1024 * 1024
        ),
        name="expert_backward",
    )(tok, w_gate, w_up, w_down, saved_gate, saved_up)


def solution(mesh):
    return jax.shard_map(
        shards,
        mesh=mesh,
        in_specs=(
            P(("group", "expert"), "tp"),
            P(("group", "expert"), None),
            P(("group", "expert"), None),
            P(("group", "expert"), None, "tp"),
            P(("group", "expert"), None, "tp"),
            P(("group", "expert"), "tp", None),
            P(("group", "expert"), "tp"),
            P(("group", "expert"), "tp"),
        ),
        out_specs=(P(("group", "expert"), "tp"), P(("group", "expert"), None)),
        check_vma=False,
    )
```

time: 355 us -> 126 us (0.35)
  the two profiles are of different devices: /device:TPU:32 before, /device:TPU:256 now
where the time goes in v1:
time: 126 us; the launch traced here: 125 us
  Pallas kernels  116 us (92%)
  local copies, waits for them, and re-layouts  8.06 us (6%)
    pallas_call x1, Pallas kernels, shards(): pl.pallas_call(functools.partial(kernel, nx, nz, width), out_shape=(jax.S...  116 us
    unnamed x16, local copies, waits for them, and re-layouts  7.24 us

profile of v1, /device:TPU:256, one launch (start us, length us, event | category | flops | bytes accessed | tf_op | source)
XLA Modules:
  0.0 125.3 jit_solution(16299268566908125115)
XLA Ops:
  0.6 0.0 copy-start.5
  0.7 0.1 pad.3.clone
  0.7 0.6 copy-done.5
  1.3 0.0 copy-start.6
  1.3 0.1 copy.13
  1.4 0.6 copy-done.6
  2.0 0.1 copy.14
  2.1 0.8 maximum_maximum_fusion.tok
  2.9 0.0 copy-start
  2.9 1.2 copy-done
  4.1 0.0 copy-start.1
  4.1 1.2 copy-done.1
  5.3 0.0 copy-start.2
  5.3 1.2 copy-done.2
  6.5 0.0 copy-start.3
  6.5 0.9 copy-done.3
  7.4 0.0 copy-start.4
  7.4 0.9 copy-done.4
  8.3 115.8 %expert_backward.1 = (f32[16,896]{1,0:T(8,128)S(1)}, f32[16,8]{1,0:T(8,128)S(1)}) custom-call(bf16[16,1024]{1,0:T(8,128)(2,1)S(1)} %maximum_maximum_fusion.tok, bf16[1,3584,128]{2,1,0:T(8,128)(2,1)S(1)} %copy-done, bf16[1,3584,128]{2,1,0:T(8,128)(2,1)S(1)} %copy-done.1, bf16[1,128,3584]{2,1,0:T(8,128)(2,1)S(1)} %copy-done.2, bf16[512,128]{1,0:T(8,128)(2,1)S(1)} %copy-done.3, ...), custom_call_target="tpu_custom_call" | custom-call | tf_op jit(solution)/shard_map/expert_backward/pallas_call | solution.py:432
  124.1 0.7 copy.15
  124.7 0.6 copy.17
  (2 shorter events, 0.0 us)
Async XLA Ops:
  0.6 0.7 copy-start.5
  1.3 0.7 copy-start.6
  2.9 1.2 copy-start
  4.1 1.2 copy-start.1
  5.3 1.2 copy-start.2
  6.5 0.9 copy-start.3
  7.4 0.9 copy-start.4

commit v2 on v1

v2 whole, which is shorter than its diff:
```python
import functools

import jax
import jax.numpy as jnp
from jax import lax
from jax.experimental import pallas as pl
from jax.experimental.pallas import tpu as pltpu
from jax.sharding import PartitionSpec as P

MESH = pl.DeviceIdType.MESH
F32 = jnp.float32
BF16 = jnp.bfloat16
TP = 4
TOK = 16
META = 128


def dot_nn(left, right):
    return lax.dot_general(left, right, (((1,), (0,)), ((), ())), preferred_element_type=F32)


def dot_nt(left, right):
    return lax.dot_general(left, right, (((1,), (1,)), ((), ())), preferred_element_type=F32)


def dot_tn(left, right):
    return lax.dot_general(left, right, (((0,), (0,)), ((), ())), preferred_element_type=F32)


def rcopy(src, dst, send, recv, device):
    return pltpu.make_async_remote_copy(
        src_ref=src, dst_ref=dst, send_sem=send, recv_sem=recv, device_id=device, device_id_type=MESH
    )


def step_of(j, count):
    odd = j % 2
    return odd * ((j + 1) // 2) + (1 - odd) * ((count - j // 2) % count)


def kernel(
    nx, nz, width,
    go_hbm, ids_hbm, rw_hbm, wg_hbm, wu_hbm, wd_hbm, sg_hbm, su_hbm,
    gin_ref, grt_ref,
    tok, IDS, RW, T, SEL, SMAT, SWT, IDW, RH, WD, WG, WU, SG, SU, A1, A2, A3, TM, RT, RTS, RTR, ZTS, ZTR,
    SR, SL, RR, RL, ZS, ZRET, OUT0, OUT1, XR0, XR1, HB, HR,
    lsem, ws, wr, hs, hr, xs, xr, zs, zr, ags, agr, rss, rsr, zbs, zbr, rts, rtr, zts, ztr, xbs, xbr,
):
    g = lax.axis_index("group")
    e = lax.axis_index("expert")
    q = lax.axis_index("tp")
    h, z = g // nz, g % nz
    x, c = e // 2, e % 2
    ntok = nx * TOK
    sp = 2 * nx
    half_slots = nz * sp
    nslot = 2 * half_slots
    per_half = nz // 2
    hid = 128
    slots = 2 * nslot

    def dev_x(k):
        return {"expert": ((x + k) % nx) * 2 + c}

    def dev_z(zz):
        return {"group": h * nz + zz}

    sibling = {"expert": x * 2 + (1 - c)}
    partner = {"group": (1 - h) * nz + z}

    pairs = (
        (sg_hbm, SG.at[0], SG.at[1]),
        (su_hbm, SU.at[0], SU.at[1]),
        (wd_hbm.at[0], WD.at[pl.ds(0, hid), :], WD.at[pl.ds(hid, hid), :]),
        (wg_hbm.at[0], WG.at[:, pl.ds(0, hid)], WG.at[:, pl.ds(hid, hid)]),
        (wu_hbm.at[0], WU.at[:, pl.ds(0, hid)], WU.at[:, pl.ds(hid, hid)]),
    )
    small = [
        pltpu.make_async_copy(go_hbm, tok.at[:, pl.ds(0, width)], lsem.at[5]),
        pltpu.make_async_copy(ids_hbm, IDS, lsem.at[6]),
        pltpu.make_async_copy(rw_hbm, RW, lsem.at[7]),
    ]
    for copy in small:
        copy.start()
    local = [pltpu.make_async_copy(src, own, lsem.at[i]) for i, (src, own, _) in enumerate(pairs)]
    for copy in local:
        copy.start()

    barrier = pltpu.get_barrier_semaphore()
    for k in range(1, nx):
        pl.semaphore_signal(barrier, inc=1, device_id=dev_x(k), device_id_type=MESH)
    for k in range(1, nz):
        pl.semaphore_signal(barrier, inc=1, device_id=dev_z((z + k) % nz), device_id_type=MESH)
    for k in range(1, TP):
        pl.semaphore_signal(barrier, inc=1, device_id={"tp": (q + k) % TP}, device_id_type=MESH)
    pl.semaphore_signal(barrier, inc=1, device_id=sibling, device_id_type=MESH)
    pl.semaphore_signal(barrier, inc=1, device_id=partner, device_id_type=MESH)
    for copy in small:
        copy.wait()
    lane = lax.broadcasted_iota(jnp.int32, (8, META), 1)
    entry = lax.broadcasted_iota(jnp.int32, (8, META), 0)
    tok[:, pl.ds(width, META)] = (
        dot_tn(IDS[...].astype(F32).astype(BF16), (lane == entry).astype(F32).astype(BF16))
        + dot_tn(RW[...], (lane == entry + 8).astype(F32).astype(BF16))
    ).astype(BF16)
    pl.semaphore_wait(barrier, nx + nz + TP - 1)

    def along_x(half, k):
        src = tok if half == 0 else T.at[1, x]
        return rcopy(src, T.at[half, x], xs.at[half, k], xr.at[half, x], dev_x(k))

    def arrives_x(half, k):
        origin = (x + k) % nx
        return rcopy(tok, T.at[half, origin], xs.at[half, k], xr.at[half, origin], dev_x(k))

    to_partner = rcopy(tok, T.at[1, x], hs.at[0], hr.at[0], partner)
    to_partner.start()
    for k in range(1, nx):
        along_x(0, k).start()
    T[0, x] = tok[...]
    siblings = [rcopy(src, far, ws.at[i], wr.at[i], sibling) for i, (src, _, far) in enumerate(pairs)]
    for copy in siblings:
        copy.start()
    to_partner.wait_recv()
    for k in range(1, nx):
        along_x(1, k).start()

    for i in range(2):
        local[i].wait()
        siblings[i].wait_recv()
    rest = lax.broadcasted_iota(jnp.int32, (sp, slots), 0)
    col = lax.broadcasted_iota(jnp.int32, (sp, slots), 1)
    within = ((rest >> 1) << 2) + (rest & 1) + c * 2
    pieces = []
    for half in (h, 1 - h):
        for j in range(nz):
            first = (half * nz + (z + step_of(j, nz)) % nz) * (4 * nx)
            pieces.append((within == col - first).astype(F32))
    pick = jnp.concatenate(pieces, axis=0).astype(BF16)
    for s in range(2):
        gate = dot_nn(pick, SG[s])
        up = dot_nn(pick, SU[s])
        sigma = jax.nn.sigmoid(gate)
        act = gate * sigma
        lanes = pl.ds(s * hid, hid)
        A1[:, :, lanes] = (up * sigma * (1.0 + gate * (1.0 - sigma))).reshape(nz, 2 * sp, hid)
        A2[:, :, lanes] = act.reshape(nz, 2 * sp, hid)
        A3[:, :, lanes] = (act * up).reshape(nz, 2 * sp, hid)

    def expert_at(j):
        zz = (z + nz - step_of(j, nz)) % nz
        return ((h * nz + zz) * nx + x).astype(F32)

    def slot_rows(half, j):
        return rcopy(
            SEL.at[half, j], RH.at[q, half * per_half + j // 2, j % 2], zs.at[half, j], zr.at[half, j],
            dev_z((z + nz - step_of(j, nz)) % nz),
        )

    def choose(half):
        for k in range(1, nx):
            arrives_x(half, k).wait_recv()
        meta_t = jnp.transpose(T[half, :, :, pl.ds(width, META)].reshape(ntok, META).astype(F32))
        IDW[half] = meta_t[0:16, :]
        ids8 = IDW[half, 0:8, :]
        w8 = IDW[half, 8:16, :]
        match_rows, weight_rows = [], []
        for j in range(nz):
            hit = (ids8 == expert_at(j)).astype(F32)
            match_rows.append(jnp.sum(hit, axis=0, keepdims=True))
            weight_rows.append(jnp.sum(hit * w8, axis=0, keepdims=True))
        t_row = lax.broadcasted_iota(jnp.int32, (ntok, ntok), 0)
        t_col = lax.broadcasted_iota(jnp.int32, (ntok, ntok), 1)
        before = jnp.logical_and(t_row >> 4 == t_col >> 4, t_row < t_col).astype(F32).astype(BF16)
        matches = jnp.concatenate(match_rows, axis=0)
        ranks = dot_nn(matches.astype(BF16), before)
        s_row = lax.broadcasted_iota(jnp.int32, (sp, ntok), 0)
        s_block = (s_row >> 1 == lax.broadcasted_iota(jnp.int32, (sp, ntok), 1) >> 4).astype(F32)
        s_level = (s_row & 1).astype(F32)
        for j in range(nz):
            SMAT[half, j] = s_block * matches[j:j + 1, :] * (s_level == ranks[j:j + 1, :]).astype(F32)
        tokens = T[half, :, :, pl.ds(0, width)].reshape(ntok, width)
        selected = dot_nn(SMAT[half].reshape(half_slots, ntok).astype(BF16), tokens).astype(BF16)
        SEL[half] = selected.reshape(nz, sp, width)
        for j in range(1, nz):
            slot_rows(half, j).start()
        RH[q, half * per_half, 0] = SEL[half, 0]
        weighted = jnp.concatenate([SMAT[half, j] * weight_rows[j] for j in range(nz)], axis=0)
        SWT[half] = jnp.transpose(weighted).astype(BF16)

    choose(0)

    def spread(origin, i, way):
        return rcopy(
            RH.at[origin, i], RH.at[origin, i], ags.at[way, origin, i], agr.at[origin, i],
            {"tp": (q + 1 - 2 * way) % TP},
        )

    def passed(s, i, way):
        src, dst = ((SR, RR), (SL, RL))[way]
        return rcopy(
            src.at[s, i], dst.at[s, i], rss.at[way, s, i], rsr.at[way, s, i], {"tp": (q + 1 - 2 * way) % TP}
        )

    def back(half, j):
        return rcopy(
            ZS.at[half * per_half + j // 2, j % 2], ZRET.at[half, j], zbs.at[half, j], zbr.at[half, j],
            dev_z((z + step_of(j, nz)) % nz),
        )

    def route_tp(k):
        return rcopy(RTS, RTR.at[k - 1], rts.at[k - 1], rtr.at[k - 1], {"tp": (q + k) % TP})

    def route_z(j):
        return rcopy(ZTS, ZTR.at[j], zts.at[j], ztr.at[j], dev_z((z + step_of(j, nz)) % nz))

    def home(half, k):
        src, dst = ((OUT0, XR0), (OUT1, XR1))[half]
        return rcopy(src.at[(x + k) % nx], dst.at[k], xbs.at[half, k], xbr.at[half, k], dev_x(k))

    def combine(half):
        for j in range(1, nz):
            back(half, j).wait_recv()
        rows = ZRET[half].reshape(half_slots, width)
        return dot_nn(SWT[half], rows).astype(BF16).reshape(nx, TOK, width)

    def body(t, carry):
        @pl.when(t == min(2, per_half))
        def _():
            choose(1)

        @pl.when(t < nz)
        def _():
            half, r = t // per_half, t % per_half

            @pl.when(r > 0)
            def _():
                slot_rows(half, 2 * r).wait_recv()

            slot_rows(half, 2 * r + 1).wait_recv()

            @pl.when(q < TP - 1)
            def _():
                spread(q, t, 0).start()

            @pl.when(q > 0)
            def _():
                spread(q, t, 1).start()

        for k in range(1, TP):
            i = t - k

            @pl.when(jnp.logical_and(i >= 0, i < nz))
            def _():
                @pl.when(q >= k)
                def _():
                    spread(q - k, i, 0).wait_recv()

                    @pl.when(q < TP - 1)
                    def _():
                        spread(q - k, i, 0).start()

                @pl.when(q + k < TP)
                def _():
                    spread(q + k, i, 1).wait_recv()

                    @pl.when(q > 0)
                    def _():
                        spread(q + k, i, 1).start()

        i = t - (TP - 1)

        @pl.when(jnp.logical_and(i >= 0, i < nz))
        def _():
            @pl.when(i == 0)
            def _():
                for n in range(2, 5):
                    local[n].wait()
                    siblings[n].wait_recv()

            adjoint = dot_nt(RH[0, i].reshape(2 * sp, width), WD[:, pl.ds(0, width)])
            for s in range(1, TP):
                adjoint += dot_nt(RH[s, i].reshape(2 * sp, width), WD[:, pl.ds(s * width, width)])
            d_gate = (adjoint * A1[i]).astype(BF16)
            d_up = (adjoint * A2[i]).astype(BF16)
            RT[i] = jnp.broadcast_to(jnp.sum(adjoint * A3[i], axis=1, keepdims=True), (2 * sp, META))
            for s in range(TP):
                part = pl.ds(s * width, width)
                TM[s, i] = dot_nt(d_gate, WG[part, :]) + dot_nt(d_up, WU[part, :])

        @pl.when(t == nz + TP - 2)
        def _():
            RTS[...] = jnp.transpose(RT[...].reshape(nslot, META))[0:8, :]
            for k in range(1, TP):
                route_tp(k).start()

        for k in range(TP - 1):
            i = t - (TP - 1) - k

            @pl.when(jnp.logical_and(i >= 0, i < nz))
            def _():
                for way in range(2):
                    place = k if way == 0 else TP - 1 - k
                    src, dst = ((SR, RR), (SL, RL))[way]
                    targets = range(TP - 1, k, -1) if way == 0 else range(0, TP - 1 - k)

                    @pl.when(q == place)
                    def _():
                        for s in targets:
                            value = TM[s, i]
                            if k > 0:
                                passed(s, i, way).wait_recv()
                                value = value + dst[s, i].astype(F32)
                            src[s, i] = value.astype(BF16)
                            passed(s, i, way).start()

        i = t - 2 * (TP - 1)

        @pl.when(jnp.logical_and(i >= 0, i < nz))
        def _():
            @pl.when(q > 0)
            def _():
                passed(q, i, 0).wait_recv()
                TM[q, i] = TM[q, i] + RR[q, i].astype(F32)

            @pl.when(q < TP - 1)
            def _():
                passed(q, i, 1).wait_recv()
                TM[q, i] = TM[q, i] + RL[q, i].astype(F32)

            half, r = i // per_half, i % per_half
            ZS[i] = TM[q, i].astype(BF16).reshape(2, sp, width)
            back(half, 2 * r + 1).start()

            @pl.when(r == 0)
            def _():
                ZRET[half, 0] = ZS[i, 0]

            @pl.when(r > 0)
            def _():
                back(half, 2 * r).start()

        @pl.when(t == per_half + 2 * (TP - 1))
        def _():
            OUT0[...] = combine(0)
            for k in range(1, nx):
                home(0, k).start()

        @pl.when(t == nz + TP)
        def _():
            for k in range(1, TP):
                route_tp(k).wait_recv()
            ZTS[...] = RTS[...] + RTR[0] + RTR[1] + RTR[2]
            ZTR[0] = ZTS[...]
            for j in range(1, nz):
                route_z(j).start()

        return carry

    lax.fori_loop(0, nz + 2 * (TP - 1), body, 0)

    for j in range(1, nz):
        route_z(j).wait_recv()
    columns = jnp.transpose(ZTR[...].reshape(nz * 8, nslot))
    for half in range(2):
        ids_now = IDW[half, 0:8, :]
        route = jnp.zeros((8, ntok), F32)
        for j in range(nz):
            start = half * half_slots + j * sp
            column = columns[start:start + sp, 8 * j:8 * j + 1]
            value = jnp.sum(SMAT[half, j] * column, axis=0, keepdims=True)
            route += (ids_now == expert_at(j)).astype(F32) * value
        route_t = jnp.transpose(jnp.concatenate([route, jnp.zeros((META - 8, ntok), F32)], axis=0))
        lanes = pl.ds(width + META * (1 - half), META)
        OUT1[:, :, lanes] = route_t.astype(BF16).reshape(nx, TOK, META)
    OUT1[:, :, pl.ds(0, width)] = combine(1)
    for k in range(1, nx):
        home(1, k).start()
    near = OUT0[x].astype(F32)
    for k in range(1, nx):
        home(0, k).wait_recv()
        near += XR0[k].astype(F32)
    gin_ref[...] = near
    total = OUT1[x].astype(F32)
    for k in range(1, nx):
        home(1, k).wait_recv()
        total += XR1[k].astype(F32)
    HB[...] = total[:, 0:width + META].astype(BF16)
    homeward = rcopy(HB, HR, hs.at[1], hr.at[1], partner)
    homeward.start()
    homeward.wait_recv()
    gin_ref[...] += HR[:, pl.ds(0, width)].astype(F32)
    route_here = total[:, width + META:width + 2 * META] + HR[:, pl.ds(width, META)].astype(F32)
    grt_ref[...] = jnp.transpose(route_here)[0:8, :]

    to_partner.wait_send()
    homeward.wait_send()
    for copy in siblings:
        copy.wait_send()
    for k in range(1, TP):
        route_tp(k).wait_send()
    for half in range(2):
        for k in range(1, nx):
            along_x(half, k).wait_send()
            home(half, k).wait_send()
        for j in range(1, nz):
            slot_rows(half, j).wait_send()
            back(half, j).wait_send()
    for j in range(1, nz):
        route_z(j).wait_send()

    def drain(i, carry):
        for origin in range(TP):
            @pl.when(jnp.logical_and(q >= origin, q < TP - 1))
            def _():
                spread(origin, i, 0).wait_send()

            @pl.when(jnp.logical_and(q <= origin, q > 0))
            def _():
                spread(origin, i, 1).wait_send()

            @pl.when(q < origin)
            def _():
                passed(origin, i, 0).wait_send()

            @pl.when(q > origin)
            def _():
                passed(origin, i, 1).wait_send()

        return carry

    lax.fori_loop(0, nz, drain, 0)


def shards(grad_out, route_weights, expert_ids, w_gate, w_up, w_down, saved_gate, saved_up):
    width = grad_out.shape[1]
    nz = lax.axis_size("group") // 2
    nx = lax.axis_size("expert") // 2
    ntok, sp = nx * TOK, 2 * nx
    half_slots = nz * sp
    nslot = 2 * half_slots
    features = TP * width
    slots = saved_gate.shape[0]
    topk = expert_ids.shape[1]
    vmem = pltpu.VMEM
    dma = pltpu.SemaphoreType.DMA
    piece = (nz, 2, sp, width)
    flat = (nz, 2 * sp, width)
    wide = width + META
    scratch = [
        vmem((TOK, wide), BF16),
        vmem((topk, TOK), jnp.int32),
        vmem((topk, TOK), BF16),
        vmem((2, nx, TOK, wide), BF16),
        vmem((2, nz, sp, width), BF16),
        vmem((2, nz, sp, ntok), F32),
        vmem((2, ntok, half_slots), BF16),
        vmem((2, 16, ntok), F32),
        vmem((TP,) + piece, BF16),
        vmem((256, features), BF16),
        vmem((features, 256), BF16),
        vmem((features, 256), BF16),
        vmem((2, slots, 128), BF16),
        vmem((2, slots, 128), BF16),
        vmem((nz, 2 * sp, 256), F32),
        vmem((nz, 2 * sp, 256), F32),
        vmem((nz, 2 * sp, 256), F32),
        vmem((TP,) + flat, F32),
        vmem((nz, 2 * sp, META), F32),
        vmem((8, nslot), F32),
        vmem((TP - 1, 8, nslot), F32),
        vmem((8, nslot), F32),
        vmem((nz, 8, nslot), F32),
        vmem((TP,) + flat, BF16),
        vmem((TP,) + flat, BF16),
        vmem((TP,) + flat, BF16),
        vmem((TP,) + flat, BF16),
        vmem(piece, BF16),
        vmem((2, nz, sp, width), BF16),
        vmem((nx, TOK, width), BF16),
        vmem((nx, TOK, wide + META), BF16),
        vmem((nx, TOK, width), BF16),
        vmem((nx, TOK, wide + META), BF16),
        vmem((TOK, wide), BF16),
        vmem((TOK, wide), BF16),
        dma((8,)), dma((5,)), dma((5,)),
        dma((2,)), dma((2,)),
        dma((2, nx)), dma((2, nx)),
        dma((2, nz)), dma((2, nz)),
        dma((2, TP, nz)), dma((TP, nz)),
        dma((2, TP, nz)), dma((2, TP, nz)),
        dma((2, nz)), dma((2, nz)),
        dma((TP - 1,)), dma((TP - 1,)),
        dma((nz,)), dma((nz,)),
        dma((2, nx)), dma((2, nx)),
    ]
    whole = pl.BlockSpec(memory_space=pltpu.VMEM)
    far = pl.BlockSpec(memory_space=pltpu.HBM)
    grad_in, grad_route = pl.pallas_call(
        functools.partial(kernel, nx, nz, width),
        out_shape=(
            jax.ShapeDtypeStruct((TOK, width), F32),
            jax.ShapeDtypeStruct((topk, TOK), F32),
        ),
        in_specs=[far] * 8,
        out_specs=(whole, whole),
        scratch_shapes=scratch,
        compiler_params=pltpu.CompilerParams(
            collective_id=0, has_side_effects=True, vmem_limit_bytes=(64 * 1024 - 256) * 1024
        ),
        name="expert_backward",
    )(grad_out, expert_ids.T, route_weights.T, w_gate, w_up, w_down, saved_gate, saved_up)
    return grad_in, grad_route.T


def solution(mesh):
    return jax.shard_map(
        shards,
        mesh=mesh,
        in_specs=(
            P(("group", "expert"), "tp"),
            P(("group", "expert"), None),
            P(("group", "expert"), None),
            P(("group", "expert"), None, "tp"),
            P(("group", "expert"), None, "tp"),
            P(("group", "expert"), "tp", None),
            P(("group", "expert"), "tp"),
            P(("group", "expert"), "tp"),
        ),
        out_specs=(P(("group", "expert"), "tp"), P(("group", "expert"), None)),
        check_vma=False,
    )
```

time: 126 us -> 114 us (0.905)
  the two profiles are of different devices: /device:TPU:256 before, /device:TPU:4 now
where the time goes in v2:
time: 114 us
  Pallas kernels  111 us (97%)
  local copies, waits for them, and re-layouts  2.04 us (2%)
    pallas_call x1, Pallas kernels, shards(): pl.pallas_call(functools.partial(kernel, nx, nz, width), out_shape=(jax.S...  111 us

profile of v2, /device:TPU:4, one launch (start us, length us, event | category | flops | bytes accessed | tf_op | source)
XLA Modules:
  0.0 113.6 jit_solution(541977171588861709)
XLA Ops:
  0.6 110.9 %expert_backward.1 = (f32[16,896]{1,0:T(8,128)}, f32[8,16]{1,0:T(8,128)}) custom-call(bf16[16,896]{1,0:T(8,128)(2,1)} %go_hbm.1, s32[8,16]{1,0:T(8,128)} %bitcast.3, bf16[8,16]{1,0:T(8,128)(2,1)} %bitcast.5, bf16[1,3584,128]{2,1,0:T(8,128)(2,1)} %wg_hbm.1, bf16[1,3584,128]{2,1,0:T(8,128)(2,1)} %wu_hbm.1, bf16[1,128,3584]{2,1,0:T(8,128)(2,1)} %wd_hbm.1, ...), custom_call_target="tpu_custom_call" | custom-call | tf_op jit(solution)/shard_map/expert_backward/pallas_call | solution.py:499
  111.5 0.0 copy-start
  111.5 1.4 %copy.12 = f32[16,896]{1,0:T(8,128)} copy(f32[16,896]{1,0:T(8,128)} %get-tuple-element.8) | data formatting | bytes 114688
  113.0 0.0 copy-done
  113.0 0.6 copy.13
Async XLA Ops:
  111.5 1.5 %copy-start = (f32[8,16]{1,0:T(8,128)S(1)}, f32[8,16]{1,0:T(8,128)}, u32[]{:S(2)}) copy-start(f32[8,16]{1,0:T(8,128)} %get-tuple-element.5) | copy-start | bytes 1540

commit v3 on v2

--- a/solution.py
+++ b/solution.py
@@ -56,8 +56,18 @@
     half_slots = nz * sp
     nslot = 2 * half_slots
     per_half = nz // 2
+    lead = per_half // 2
     hid = 128
     slots = 2 * nslot
+
+    def half_of(i):
+        return ((i + lead) // per_half) % 2
+
+    def pair_of(i):
+        return (i + lead + lead * (1 - half_of(i))) % per_half
+
+    def piece_of(half, j):
+        return [i for i in range(nz) if half_of(i) == half and pair_of(i) == j // 2][0]
 
     def dev_x(k):
         return {"expert": ((x + k) % nx) * 2 + c}
@@ -132,8 +142,9 @@
     col = lax.broadcasted_iota(jnp.int32, (sp, slots), 1)
     within = ((rest >> 1) << 2) + (rest & 1) + c * 2
     pieces = []
-    for half in (h, 1 - h):
-        for j in range(nz):
+    for i in range(nz):
+        half = (h, 1 - h)[half_of(i)]
+        for j in (2 * pair_of(i), 2 * pair_of(i) + 1):
             first = (half * nz + (z + step_of(j, nz)) % nz) * (4 * nx)
             pieces.append((within == col - first).astype(F32))
     pick = jnp.concatenate(pieces, axis=0).astype(BF16)
@@ -151,9 +162,10 @@
         zz = (z + nz - step_of(j, nz)) % nz
         return ((h * nz + zz) * nx + x).astype(F32)
 
-    def slot_rows(half, j):
+    def slot_rows(half, j, i=None):
+        i = piece_of(half, j) if i is None else i
         return rcopy(
-            SEL.at[half, j], RH.at[q, half * per_half + j // 2, j % 2], zs.at[half, j], zr.at[half, j],
+            SEL.at[half, j], RH.at[q, i, j % 2], zs.at[half, j], zr.at[half, j],
             dev_z((z + nz - step_of(j, nz)) % nz),
         )
 
@@ -184,7 +196,7 @@
         SEL[half] = selected.reshape(nz, sp, width)
         for j in range(1, nz):
             slot_rows(half, j).start()
-        RH[q, half * per_half, 0] = SEL[half, 0]
+        RH[q, piece_of(half, 0), 0] = SEL[half, 0]
         weighted = jnp.concatenate([SMAT[half, j] * weight_rows[j] for j in range(nz)], axis=0)
         SWT[half] = jnp.transpose(weighted).astype(BF16)
 
@@ -202,17 +214,49 @@
             src.at[s, i], dst.at[s, i], rss.at[way, s, i], rsr.at[way, s, i], {"tp": (q + 1 - 2 * way) % TP}
         )
 
-    def back(half, j):
+    def back(half, j, i=None):
+        i = piece_of(half, j) if i is None else i
         return rcopy(
-            ZS.at[half * per_half + j // 2, j % 2], ZRET.at[half, j], zbs.at[half, j], zbr.at[half, j],
+            ZS.at[i, j % 2], ZRET.at[half, j], zbs.at[half, j], zbr.at[half, j],
             dev_z((z + step_of(j, nz)) % nz),
         )
 
-    def route_tp(k):
-        return rcopy(RTS, RTR.at[k - 1], rts.at[k - 1], rtr.at[k - 1], {"tp": (q + k) % TP})
-
-    def route_z(j):
-        return rcopy(ZTS, ZTR.at[j], zts.at[j], ztr.at[j], dev_z((z + step_of(j, nz)) % nz))
+    def route_tp(half, k):
+        return rcopy(
+            RTS.at[half], RTR.at[half, k - 1], rts.at[half, k - 1], rtr.at[half, k - 1], {"tp": (q + k) % TP}
+        )
+
+    def route_z(half, j):
+        return rcopy(
+            ZTS.at[half], ZTR.at[half, j], zts.at[half, j], ztr.at[half, j], dev_z((z + step_of(j, nz)) % nz)
+        )
+
+    def route_out(half):
+        parts = [RT[piece_of(half, 2 * r)] for r in range(per_half)]
+        RTS[half] = jnp.transpose(jnp.concatenate(parts, axis=0))[0:8, :]
+        for k in range(1, TP):
+            route_tp(half, k).start()
+
+    def route_on(half):
+        for k in range(1, TP):
+            route_tp(half, k).wait_recv()
+        ZTS[half] = RTS[half] + RTR[half, 0] + RTR[half, 1] + RTR[half, 2]
+        ZTR[half, 0] = ZTS[half]
+        for j in range(1, nz):
+            route_z(half, j).start()
+
+    def route_back(half):
+        for j in range(1, nz):
+            route_z(half, j).wait_recv()
+        columns = jnp.transpose(ZTR[half].reshape(nz * 8, half_slots))
+        ids_now = IDW[half, 0:8, :]
+        route = jnp.zeros((8, ntok), F32)
+        for j in range(nz):
+            column = columns[j * sp:(j + 1) * sp, 8 * j:8 * j + 1]
+            value = jnp.sum(SMAT[half, j] * column, axis=0, keepdims=True)
+            route += (ids_now == expert_at(j)).astype(F32) * value
+        route_t = jnp.transpose(jnp.concatenate([route, jnp.zeros((META - 8, ntok), F32)], axis=0))
+        return route_t.astype(BF16).reshape(nx, TOK, META)
 
     def home(half, k):
         src, dst = ((OUT0, XR0), (OUT1, XR1))[half]
@@ -225,19 +269,19 @@
         return dot_nn(SWT[half], rows).astype(BF16).reshape(nx, TOK, width)
 
     def body(t, carry):
-        @pl.when(t == min(2, per_half))
+        @pl.when(t == lead)
         def _():
             choose(1)
 
         @pl.when(t < nz)
         def _():
-            half, r = t // per_half, t % per_half
+            half, r = half_of(t), pair_of(t)
 
             @pl.when(r > 0)
             def _():
-                slot_rows(half, 2 * r).wait_recv()
-
-            slot_rows(half, 2 * r + 1).wait_recv()
+                slot_rows(half, 2 * r, t).wait_recv()
+
+            slot_rows(half, 2 * r + 1, t).wait_recv()
 
             @pl.when(q < TP - 1)
             def _():
@@ -290,9 +334,11 @@
 
         @pl.when(t == nz + TP - 2)
         def _():
-            RTS[...] = jnp.transpose(RT[...].reshape(nslot, META))[0:8, :]
-            for k in range(1, TP):
-                route_tp(k).start()
+            route_out(0)
+
+        @pl.when(t == lead + per_half + TP - 2)
+        def _():
+            route_out(1)
 
         for k in range(TP - 1):
             i = t - (TP - 1) - k
@@ -328,9 +374,9 @@
                 passed(q, i, 1).wait_recv()
                 TM[q, i] = TM[q, i] + RL[q, i].astype(F32)
 
-            half, r = i // per_half, i % per_half
+            half, r = half_of(i), pair_of(i)
             ZS[i] = TM[q, i].astype(BF16).reshape(2, sp, width)
-            back(half, 2 * r + 1).start()
+            back(half, 2 * r + 1, i).start()
 
             @pl.when(r == 0)
             def _():
@@ -338,76 +384,61 @@
 
             @pl.when(r > 0)
             def _():
-                back(half, 2 * r).start()
-
-        @pl.when(t == per_half + 2 * (TP - 1))
-        def _():
-            OUT0[...] = combine(0)
+                back(half, 2 * r, i).start()
+
+        @pl.when(t == lead + per_half + TP)
+        def _():
+            route_on(1)
+
+        @pl.when(t == nz + TP)
+        def _():
+            route_on(0)
+
+        @pl.when(t == min(lead + per_half + 2 * (TP - 1), nz + 2 * (TP - 1) - 1))
+        def _():
+            OUT1[:, :, pl.ds(width, META)] = route_back(1)
+            OUT1[:, :, pl.ds(0, width)] = combine(1)
             for k in range(1, nx):
-                home(0, k).start()
-
-        @pl.when(t == nz + TP)
-        def _():
-            for k in range(1, TP):
-                route_tp(k).wait_recv()
-            ZTS[...] = RTS[...] + RTR[0] + RTR[1] + RTR[2]
-            ZTR[0] = ZTS[...]
-            for j in range(1, nz):
-                route_z(j).start()
+                home(1, k).start()
 
         return carry
 
     lax.fori_loop(0, nz + 2 * (TP - 1), body, 0)
 
-    for j in range(1, nz):
-        route_z(j).wait_recv()
-    columns = jnp.transpose(ZTR[...].reshape(nz * 8, nslot))
-    for half in range(2):
-        ids_now = IDW[half, 0:8, :]
-        route = jnp.zeros((8, ntok), F32)
-        for j in range(nz):
-            start = half * half_slots + j * sp
-            column = columns[start:start + sp, 8 * j:8 * j + 1]
-            value = jnp.sum(SMAT[half, j] * column, axis=0, keepdims=True)
-            route += (ids_now == expert_at(j)).astype(F32) * value
-        route_t = jnp.transpose(jnp.concatenate([route, jnp.zeros((META - 8, ntok), F32)], axis=0))
-        lanes = pl.ds(width + META * (1 - half), META)
-        OUT1[:, :, lanes] = route_t.astype(BF16).reshape(nx, TOK, META)
-    OUT1[:, :, pl.ds(0, width)] = combine(1)
+    OUT0[:, :, pl.ds(width, META)] = route_back(0)
+    OUT0[:, :, pl.ds(0, width)] = combine(0)
     for k in range(1, nx):
-        home(1, k).start()
+        home(0, k).start()
+    total = OUT1[x].astype(F32)
+    for k in range(1, nx):
+        home(1, k).wait_recv()
+        total += XR1[k].astype(F32)
+    HB[...] = total.astype(BF16)
+    homeward = rcopy(HB, HR, hs.at[1], hr.at[1], partner)
+    homeward.start()
     near = OUT0[x].astype(F32)
     for k in range(1, nx):
         home(0, k).wait_recv()
         near += XR0[k].astype(F32)
-    gin_ref[...] = near
-    total = OUT1[x].astype(F32)
-    for k in range(1, nx):
-        home(1, k).wait_recv()
-        total += XR1[k].astype(F32)
-    HB[...] = total[:, 0:width + META].astype(BF16)
-    homeward = rcopy(HB, HR, hs.at[1], hr.at[1], partner)
-    homeward.start()
     homeward.wait_recv()
-    gin_ref[...] += HR[:, pl.ds(0, width)].astype(F32)
-    route_here = total[:, width + META:width + 2 * META] + HR[:, pl.ds(width, META)].astype(F32)
-    grt_ref[...] = jnp.transpose(route_here)[0:8, :]
+    near += HR[...].astype(F32)
+    gin_ref[...] = near[:, 0:width]
+    grt_ref[...] = jnp.transpose(near[:, width:width + META])[0:8, :]
 
     to_partner.wait_send()
     homeward.wait_send()
     for copy in siblings:
         copy.wait_send()
-    for k in range(1, TP):
-        route_tp(k).wait_send()
     for half in range(2):
+        for k in range(1, TP):
+            route_tp(half, k).wait_send()
         for k in range(1, nx):
             along_x(half, k).wait_send()
             home(half, k).wait_send()
         for j in range(1, nz):
             slot_rows(half, j).wait_send()
             back(half, j).wait_send()
-    for j in range(1, nz):
-        route_z(j).wait_send()
+            route_z(half, j).wait_send()
 
     def drain(i, carry):
         for origin in range(TP):
@@ -467,20 +498,20 @@
         vmem((nz, 2 * sp, 256), F32),
         vmem((TP,) + flat, F32),
         vmem((nz, 2 * sp, META), F32),
-        vmem((8, nslot), F32),
-        vmem((TP - 1, 8, nslot), F32),
-        vmem((8, nslot), F32),
-        vmem((nz, 8, nslot), F32),
+        vmem((2, 8, half_slots), F32),
+        vmem((2, TP - 1, 8, half_slots), F32),
+        vmem((2, 8, half_slots), F32),
+        vmem((2, nz, 8, half_slots), F32),
         vmem((TP,) + flat, BF16),
         vmem((TP,) + flat, BF16),
         vmem((TP,) + flat, BF16),
         vmem((TP,) + flat, BF16),
         vmem(piece, BF16),
         vmem((2, nz, sp, width), BF16),
-        vmem((nx, TOK, width), BF16),
-        vmem((nx, TOK, wide + META), BF16),
-        vmem((nx, TOK, width), BF16),
-        vmem((nx, TOK, wide + META), BF16),
+        vmem((nx, TOK, wide), BF16),
+        vmem((nx, TOK, wide), BF16),
+        vmem((nx, TOK, wide), BF16),
+        vmem((nx, TOK, wide), BF16),
         vmem((TOK, wide), BF16),
         vmem((TOK, wide), BF16),
         dma((8,)), dma((5,)), dma((5,)),
@@ -490,8 +521,8 @@
         dma((2, TP, nz)), dma((TP, nz)),
         dma((2, TP, nz)), dma((2, TP, nz)),
         dma((2, nz)), dma((2, nz)),
-        dma((TP - 1,)), dma((TP - 1,)),
-        dma((nz,)), dma((nz,)),
+        dma((2, TP - 1)), dma((2, TP - 1)),
+        dma((2, nz)), dma((2, nz)),
         dma((2, nx)), dma((2, nx)),
     ]
     whole = pl.BlockSpec(memory_space=pltpu.VMEM)

time: 114 us -> 111 us (0.974)
  Pallas kernels: 111 us -> 108 us
    pallas_call x1, Pallas kernels: 111 us -> 108 us  [shards(): pl.pallas_call(functools.partial(kernel, nx, nz, width), out_shape=(jax.S...]
where the time goes in v3:
time: 111 us; the launch traced here: 110 us
  Pallas kernels  108 us (97%)
  local copies, waits for them, and re-layouts  2.04 us (2%)
    pallas_call x1, Pallas kernels, shards(): pl.pallas_call(functools.partial(kernel, nx, nz, width), out_shape=(jax.S...  108 us

profile of v3, /device:TPU:4, one launch (start us, length us, event | category | flops | bytes accessed | tf_op | source)
XLA Modules:
  0.0 110.4 jit_solution(11399874519426702123)
XLA Ops:
  0.6 107.7 %expert_backward.1 = (f32[16,896]{1,0:T(8,128)}, f32[8,16]{1,0:T(8,128)}) custom-call(bf16[16,896]{1,0:T(8,128)(2,1)} %go_hbm.1, s32[8,16]{1,0:T(8,128)} %bitcast.3, bf16[8,16]{1,0:T(8,128)(2,1)} %bitcast.5, bf16[1,3584,128]{2,1,0:T(8,128)(2,1)} %wg_hbm.1, bf16[1,3584,128]{2,1,0:T(8,128)(2,1)} %wu_hbm.1, bf16[1,128,3584]{2,1,0:T(8,128)(2,1)} %wd_hbm.1, ...), custom_call_target="tpu_custom_call" | custom-call | tf_op jit(solution)/shard_map/expert_backward/pallas_call | solution.py:530
  108.3 0.0 copy-start
  108.4 1.4 %copy.12 = f32[16,896]{1,0:T(8,128)} copy(f32[16,896]{1,0:T(8,128)} %get-tuple-element.8) | data formatting | bytes 114688
  109.8 0.0 copy-done
  109.8 0.6 copy.13
Async XLA Ops:
  108.3 1.5 %copy-start = (f32[8,16]{1,0:T(8,128)S(1)}, f32[8,16]{1,0:T(8,128)}, u32[]{:S(2)}) copy-start(f32[8,16]{1,0:T(8,128)} %get-tuple-element.5) | copy-start | bytes 1540
